TPU v7x, 32 devices: a whole 2x2x4 slice. The times are simulated.
32 devices in a mesh: groups: 2 (over x), tile: 16 (over z, y, core).
Axes of the slice: x: 2, y: 2, z: 4, core: 2. Of those that a mesh axis runs over, the one named last changes fastest.
Arguments:
- spectrum: float32 [40, 36, 32, 128], P(None, None, ('groups', 'tile')), parts along dimension 2, may hold values from 0 to 1
- sea_mask: int32 [32, 128], P(('groups', 'tile')), parts along dimension 0, may hold values from 0 to 1, as said below
- card_deal: int32 [32, 128], P(('groups', 'tile')), parts along dimension 0, may hold values from -1 to 255, as said below
- wind: float32 [2, 32, 128], P(None, ('groups', 'tile')), parts along dimension 1, may hold values from -5 to 5
Outputs:
- spectrum_out: float32 [40, 36, 32, 128], P(None, None, ('groups', 'tile')), parts along dimension 2
- card_energy: float32 [512], P(('groups', 'tile')), parts along dimension 0
There are 2 independent parts, one for each index of `groups`. A program takes and returns all parts, laid end to end along the dimension named above; each array names one. Nothing has to cross between parts.
Inputs may be any that keep to these rules, and one draw needn't show every extreme that they name: `sea_mask`: each row is sea (1) from its first cell up to a coastline and land (0) beyond. One tile of 1 row, placed by the seed, is all sea; the other tiles hold 8 times q or q + 1 sea points each, q = r // 15 with r = 16 (8) / 8, so that the window holds 256 sea points; within a tile the rows' sea counts differ by at most one, the first rows holding more. `card_deal`: land cells hold -1. Sea cells, numbered i = 0, 1, ... in row-major order over the window, hold c * 16 + s with card c = (i + o) mod 16 for an offset o drawn from the seed and slot s = i // 16. Every card holds exactly 16 points, and at most 8 points of one tile, a count that the all-sea tile reaches on every card.
All inputs are finite; a program needn't handle non-finite values.
Results may differ from a plain program's by a relative error of at most 0.0001.
Values sent between devices are 32-bit elements; how exact they have to be, the bound alone decides.
No kernel may reach another device: no remote copies, remote signals or barrier semaphores. Data moves between devices by JAX's collectives and lax.ppermute only.
A program may use at most 64 MiB of HBM per device.

v0:
```python
import functools
import math

import jax
import jax.numpy as jnp
import numpy as np
from jax import lax
from jax.experimental import pallas as pl
from jax.experimental.pallas import tpu as pltpu
from jax.sharding import PartitionSpec as P

STEPS = 2
SUB = 8
COURANT_TOP = 0.7
WIND_RATE = 0.15
DECAY_RATE = 0.3
QUAD_RATE = 0.5
LIMITER = 0.25
ANGLE_UP = -11.48
ANGLE_DOWN = 33.56
SHIFT_UP = math.log(1.25) / math.log(1.1)
SHIFT_DOWN = math.log(0.75) / math.log(1.1)
GAIN_UP = 1.25 ** (-4)
GAIN_DOWN = 0.75 ** (-4)
GAIN_BOTH = 0.9375 ** (-4)

LANES = 128
ROWS = 8
PAD = 4


def split(offset):
    base = math.floor(offset)
    return base, offset - base


GAIN = 2.0 * GAIN_BOTH / (GAIN_UP * GAIN_DOWN)
STATE = SUB / LIMITER
UP_K, UP_W = split(SHIFT_UP)
DOWN_K, DOWN_W = split(SHIFT_DOWN)

COAST = 16
NEAR = 42
REST = 14
FAR = COAST + REST + NEAR


class Pack:
    def __init__(self, blocks, width, dir_count, offset):
        self.blocks, self.width, self.offset = blocks, width, offset
        self.slabs = dir_count // blocks
        self.dir_count = dir_count

    def direction(self, block, slab):
        return (block * self.slabs + slab + self.offset) % self.dir_count

    def find(self, j):
        return divmod((j - self.offset) % self.dir_count, self.slabs)

    def next_block(self, value, lane):
        if self.blocks * self.width == LANES:
            return turn(value, -self.width)
        last = (self.blocks - 1) * self.width
        return jnp.take_along_axis(value, jnp.where(lane < last, lane + self.width, lane - last), axis=1)

    def block_before(self, value, lane):
        if self.blocks * self.width == LANES:
            return turn(value, self.width)
        last = (self.blocks - 1) * self.width
        source = jnp.where(lane >= self.width, lane - self.width, lane + last)
        return jnp.take_along_axis(value, jnp.minimum(source, LANES - 1), axis=1)

    def over_blocks(self, value, lane):
        if self.blocks == 4:
            value = value + turn(value, 2 * self.width)
            return value + turn(value, self.width)
        total = value
        for b in range(1, self.blocks):
            total = total + turn(value, -b * self.width)
        spread = total
        for b in range(1, self.blocks):
            spread = jnp.where(lane >= b * self.width, turn(total, b * self.width), spread)
        return spread

    def rows(self):
        angles = 2.0 * math.pi * np.arange(self.dir_count) / self.dir_count
        out = np.zeros((4, self.slabs, LANES))
        for r in range(self.slabs):
            for b in range(self.blocks):
                at = slice(b * self.width, (b + 1) * self.width)
                angle = angles[self.direction(b, r)]
                out[:, r, at] = np.array(
                    [math.cos(angle), math.sin(angle), abs(math.cos(angle)), abs(math.sin(angle))]
                )[:, None]
        return np.broadcast_to(out[:, :, None, :], (4, self.slabs, ROWS, LANES)).astype(np.float32)


def turn(value, by):
    by %= LANES
    return pltpu.roll(value, by, 1) if by else value


def lanes():
    return lax.broadcasted_iota(jnp.int32, (ROWS, LANES), 1)


def every_row(value, row):
    return jnp.broadcast_to(value[row:row + 1, :], (ROWS, LANES))


def within(lane, first, count):
    return (lane >= first) & (lane < first + count)


def sine_up(j, dir_count):
    return math.sin(2.0 * math.pi * j / dir_count) > 0


def tables(freq_count, dir_count):
    levels = 3.0 ** (np.arange(freq_count) / (freq_count - 1))
    speeds = COURANT_TOP * 1.1 ** (-np.arange(freq_count, dtype=np.float64))
    up_j, up_z = split(ANGLE_UP * dir_count / 360.0)
    rate = (1.0 - UP_W) * up_z / LIMITER
    rows = [
        speeds,
        rate * QUAD_RATE / (GAIN * STATE ** 3) * levels,
        WIND_RATE * 0.5 / (LIMITER * STATE) * levels,
        levels / (dir_count * np.sum(levels) * STATE),
        DECAY_RATE / (LIMITER * STATE) * levels,
    ]
    return np.broadcast_to(
        np.stack(rows)[:, :, None], (len(rows), freq_count, LANES)
    ).astype(np.float32)


def clear(ref, slabs, freq_count):
    zero = jnp.zeros((PAD, LANES), jnp.float32)
    for r in range(slabs):
        ref[r, pl.ds(0, PAD), :] = zero
        ref[r, pl.ds(PAD + freq_count, PAD), :] = zero


def set_wind(pack, freq_count, table_ref, angle_ref, aux, w_ref):
    east, north = every_row(aux, 0), every_row(aux, 1)
    for r in range(pack.slabs):
        drive = east * angle_ref[0, r] + north * angle_ref[1, r]
        for kb in range(freq_count // ROWS):
            at = pl.ds(kb * ROWS, ROWS)
            w_ref[r, at, :] = jnp.maximum(table_ref[2, at, :] * drive - WIND_RATE / (LIMITER * STATE), 0.0)


def sub_steps(pack, freq_count, table_ref, e_ref, u_ref, d_ref, n_ref, w_ref, acc_ref, c_ref):
    slabs, blocks = pack.slabs, freq_count // ROWS
    lane = lanes()
    up_j, up_z = split(ANGLE_UP * pack.dir_count / 360.0)
    down_j, down_z = split(ANGLE_DOWN * pack.dir_count / 360.0)
    up_near, up_far = up_j + 1, up_j
    up_weight, up_rest = up_z, (1.0 - up_z) / up_z
    down_near, down_far = down_j, down_j + 1
    down_weight, down_rest = 1.0 - down_z, down_z / (1.0 - down_z)
    up_scale = GAIN_UP * GAIN * up_weight
    down_scale = GAIN_DOWN * GAIN * down_weight
    fold = (1.0 - UP_W) * up_weight
    up_tail = UP_W / (1.0 - UP_W)
    down_head = (1.0 - DOWN_W) * down_weight / fold
    down_tail = DOWN_W * down_weight / fold
    own = -2.0 / fold

    def around(known, make, r):
        if r not in known:
            if r < 0:
                known[r] = pack.block_before(around(known, make, r + slabs), lane)
            elif r >= slabs:
                known[r] = pack.next_block(around(known, make, r - slabs), lane)
            else:
                known[r] = make(r)
        return known[r]

    def stage_a(kb):
        base = kb * ROWS
        strength = table_ref[1, pl.ds(base, ROWS), :]
        up, down, more, less, up_c, down_c, centre = {}, {}, {}, {}, {}, {}, {}

        def read(r, offset):
            return e_ref[r, pl.ds(base + PAD + offset, ROWS), :]

        def make_up(r):
            return (up_scale * (1.0 - UP_W)) * read(r, UP_K) + (up_scale * UP_W) * read(r, UP_K + 1)

        def make_down(r):
            return (down_scale * (1.0 - DOWN_W)) * read(r, DOWN_K) + (down_scale * DOWN_W) * read(r, DOWN_K + 1)

        def get_up(r):
            return around(up, make_up, r)

        def get_down(r):
            return around(down, make_down, r)

        def get_up_c(r):
            if r not in up_c:
                up_c[r] = get_up(r) * up_rest
            return up_c[r]

        def get_down_c(r):
            if r not in down_c:
                down_c[r] = get_down(r) * down_rest
            return down_c[r]

        def make_quad(r, sign):
            if r not in centre:
                here = read(r, 0)
                centre[r] = here, here * strength
            here, gain = centre[r]
            plus = get_up(r + sign * up_near) + get_up_c(r + sign * up_far)
            minus = get_down(r + sign * down_near) + get_down_c(r + sign * down_far)
            return gain * (here * (plus + minus) - plus * minus)

        def get_more(r):
            return around(more, lambda r: make_quad(r, 1), r)

        def get_less(r):
            return around(less, lambda r: make_quad(r, -1), r)

        if slabs > 9:
            for r in (slabs - 2, slabs - 1, 0, 1):
                get_up(r)
            for r in (*range(slabs - 4, slabs), *range(4)):
                get_down(r)
            for r in (-2, -1, slabs, slabs + 1):
                get_up(r)
            for r in (*range(-4, 0), *range(slabs, slabs + 4)):
                get_down(r)
            for r in (*range(slabs - 4, slabs), 0, 1):
                get_more(r)
            for r in (slabs - 2, slabs - 1, *range(4)):
                get_less(r)
            for r in (*range(-4, 0), slabs, slabs + 1):
                get_more(r)
            for r in (-2, -1, *range(slabs, slabs + 4)):
                get_less(r)
            order = (*range(4, slabs - 4), *range(4), *range(slabs - 4, slabs))
        else:
            order = range(slabs)
        for r in order:
            u_ref[r, pl.ds(base + PAD, ROWS), :] = (
                get_more(r - up_near) + get_less(r + up_near)
            ) + up_rest * (get_more(r - up_far) + get_less(r + up_far))
            d_ref[r, pl.ds(base + PAD, ROWS), :] = (
                get_more(r - down_near) + get_less(r + down_near)
            ) + down_rest * (get_more(r - down_far) + get_less(r + down_far))
            n_ref[r, pl.ds(base, ROWS), :] = own * (get_more(r) + get_less(r))

    def stage_b(kb):
        base = kb * ROWS
        decay = c_ref[pl.ds(base, ROWS), :]
        total = jnp.zeros((ROWS, LANES), jnp.float32)
        for r in range(slabs):
            here = e_ref[r, pl.ds(base + PAD, ROWS), :]
            rate = here * (w_ref[r, pl.ds(base, ROWS), :] - decay) + n_ref[r, pl.ds(base, ROWS), :]
            rate = rate + (
                u_ref[r, pl.ds(base + PAD - UP_K, ROWS), :]
                + up_tail * u_ref[r, pl.ds(base + PAD - UP_K - 1, ROWS), :]
            )
            rate = rate + (
                down_head * d_ref[r, pl.ds(base + PAD - DOWN_K, ROWS), :]
                + down_tail * d_ref[r, pl.ds(base + PAD - DOWN_K - 1, ROWS), :]
            )
            here = here + jnp.tanh(rate)
            e_ref[r, pl.ds(base + PAD, ROWS), :] = here
            total = total + here
        acc_ref[pl.ds(base, ROWS), :] = total

    def sub_step(index, carry):
        steepness = jnp.sum(acc_ref[...] * table_ref[3], axis=0, keepdims=True)
        steepness = pack.over_blocks(jnp.broadcast_to(steepness, (ROWS, LANES)), lane)[0:1]
        c_ref[...] = steepness * table_ref[4]
        for kb in range(blocks):
            stage_a(kb)
        for kb in range(blocks):
            stage_b(kb)
        return carry

    lax.fori_loop(0, SUB, sub_step, 0)


def slab_at(r, kb, freq_count):
    return pl.ds(r * freq_count + kb * ROWS, ROWS)


SQUEEZE = (0, COAST, 4 * COAST, 5 * COAST)


def flow_mask(lane, width, wanted):
    block = lane // width
    forward = ((block == 0) | (block == 3)).astype(jnp.int32)
    return (forward == wanted) & (lane % width < COAST)


def squeeze(fetch, count, chosen):
    out = []
    for start in range(0, count, len(SQUEEZE)):
        total = None
        for i in range(start, min(count, start + len(SQUEEZE))):
            value = turn(jnp.where(chosen, fetch(i), 0.0), SQUEEZE[i - start])
            total = value if total is None else total + value
        out.append(total)
    return out


def loosen(ref, i):
    g, part = divmod(i, len(SQUEEZE))
    return turn(ref[pl.ds(g * ROWS, ROWS), :], -SQUEEZE[part])


def in_stages(groups, stages):
    held = {}
    for t in range(len(groups) + len(stages) - 1):
        for i in reversed(range(len(stages))):
            g = t - i
            if 0 <= g < len(groups):
                held[g] = stages[i](*groups[g], *held.pop(g, ()))


def unpack_turn(value, pack):
    return turn(value, -pack.width)


def near_kernel(one, freq_count, spec_ref, own_ref, send_ref):
    dir_count = one.dir_count
    blocks = freq_count // ROWS
    chunk = ROWS * dir_count
    lane = lanes()
    angles = 2.0 * math.pi * np.arange(dir_count) / dir_count
    first = COAST + REST
    row = lax.broadcasted_iota(jnp.int32, (ROWS, LANES), 0)
    speeds = [
        COURANT_TOP * STATE * jnp.exp((row + kb * ROWS).astype(jnp.float32) * (-math.log(1.1))) for kb in range(blocks)
    ]
    groups = [(kb, range(some, some + 4)) for kb in range(blocks) for some in range(0, one.slabs, 4)]

    def read(kb, slabs):
        here, along = {}, {}
        for r in slabs:
            for b in range(one.blocks):
                j = one.direction(b, r)
                here[r, b] = spec_ref[pl.ds(kb * chunk + j, ROWS, stride=dir_count), :]
        for r, b in here:
            if sine_up(one.direction(b, r), dir_count):
                along[r, b] = turn(here[r, b], 1)
            else:
                along[r, b] = jnp.where(lane == LANES - 1, 0.0, turn(here[r, b], -1))
        return here, along

    def move(kb, slabs, here, along):
        moved = {}
        for r, b in here:
            angle = angles[one.direction(b, r)]
            cosine, sine = float(abs(math.cos(angle))), float(abs(math.sin(angle)))
            value = here[r, b] * (STATE - speeds[kb] * (cosine + sine)) + along[r, b] * (speeds[kb] * sine)
            moved[r, b] = turn(value, b * one.width - first)
        return (moved,)

    def choose(kb, slabs, moved):
        own, sent = {}, {}
        for r in slabs:
            own[r] = sent[r] = moved[r, 0]
            for b in range(1, one.blocks):
                at = b * one.width
                ahead = (at + one.width) % LANES
                own[r] = jnp.where(lane >= at, moved[r, b], own[r])
                reached = lane >= ahead
                if b == one.blocks - 1:
                    reached = reached | (lane < one.width - (LANES - ahead))
                sent[r] = jnp.where(reached, moved[r, b], sent[r])
        return own, {r: unpack_turn(sent[r], one) for r in slabs}

    def store(kb, slabs, own, sent):
        for r in slabs:
            own_ref[slab_at(r, kb, freq_count), :] = own[r]
            send_ref[slab_at(r, kb, freq_count), :] = sent[r]

    in_stages(groups, (read, move, choose, store))


def pack_aux(pack, aux, first, slot, count):
    lane = lanes()
    total = jnp.zeros((ROWS, LANES), jnp.float32)
    for b in range(pack.blocks):
        at = b * pack.width + slot
        total = jnp.where(within(lane, at, count), turn(aux, at - first), total)
    return total


def aux_kernel(one, two, mask_ref, wind_ref, deal_ref, row_ref, own_ref, send_ref):
    mask = mask_ref[...].astype(jnp.float32)
    aux = jnp.concatenate(
        [
            wind_ref[...] * mask,
            (deal_ref[...] + 1).astype(jnp.float32) * mask,
            mask,
            jnp.zeros((ROWS - 4, LANES), jnp.float32),
        ],
        axis=0,
    )
    row_ref[...] = jnp.concatenate(
        [mask, jnp.broadcast_to(mask[:, LANES - 1:LANES], (1, LANES)), jnp.zeros((ROWS - 2, LANES), jnp.float32)], axis=0
    )
    own_ref[pl.ds(0, ROWS), :] = pack_aux(one, aux, COAST + REST, 0, NEAR)
    own_ref[pl.ds(ROWS, ROWS), :] = pack_aux(two, aux, 0, 0, COAST + REST)
    send_ref[pl.ds(0, ROWS), :] = pack_aux(one, aux, FAR, 0, NEAR)
    send_ref[pl.ds(ROWS, ROWS), :] = pack_aux(two, aux, FAR + NEAR, COAST, REST)


def coast_kernel(two, freq_count, code_ref, spec_ref, row_ref, own_ref, send_ref, cross_ref):
    dir_count = two.dir_count
    blocks = freq_count // ROWS
    chunk = ROWS * dir_count
    lane = lanes()
    slot = lane % two.width
    mask = every_row(row_ref[...], 0)
    for kb in range(blocks):
        done = []
        for r in range(two.slabs):
            own, sent = None, None
            for b in range(two.blocks):
                j = two.direction(b, r)
                here = spec_ref[pl.ds(kb * chunk + j, ROWS, stride=dir_count), :] * mask
                here = turn(here, b * two.width)
                block = within(lane, b * two.width, two.width)
                behind = within(lane, (b - 1) % two.blocks * two.width, two.width)
                own = here if b == 0 else jnp.where(block, here, own)
                sent = here if b == 0 else jnp.where(behind, here, sent)
            done.append((own, jnp.where(slot < COAST, own, sent)))
        for r, (own, sent) in enumerate(done):
            own_ref[slab_at(r, kb, freq_count), :] = own
            send_ref[slab_at(r, kb, freq_count), :] = sent

    chosen = flow_mask(lane, two.width, code_ref[0] % 2)
    for g, value in enumerate(squeeze(lambda i: own_ref[pl.ds(i * ROWS, ROWS), :], two.slabs * blocks, chosen)):
        cross_ref[pl.ds(g * ROWS, ROWS), :] = value


NEAR_ENDS = NEAR - 1, 0
REST_ENDS = COAST + REST - 1, COAST


def end_lane(pack, j, ends):
    return pack.find(j)[0] * pack.width + ends[0 if sine_up(j, pack.dir_count) else 1]


def column_lane(one, j):
    return (end_lane(one, j, NEAR_ENDS) + 2 * one.find(j)[1] - 30) % LANES


def take_column(one, pack, ends, fetch, lane):
    total = jnp.zeros((ROWS, LANES), jnp.float32)
    values = [fetch(r) for r in range(pack.slabs)]
    for r, value in enumerate(values):
        turned = {}
        for b in range(pack.blocks):
            j = pack.direction(b, r)
            to = column_lane(one, j)
            by = (to - end_lane(pack, j, ends)) % LANES
            if by not in turned:
                turned[by] = turn(value, by)
            total = jnp.where(lane == to, turned[by], total)
    return total


def store_state(pack, freq_count, e_ref, scale, out_ref):
    for r in range(pack.slabs):
        blocks = range(freq_count // ROWS)
        done = [e_ref[r, pl.ds(PAD + kb * ROWS, ROWS), :] * scale for kb in blocks]
        for kb in blocks:
            out_ref[slab_at(r, kb, freq_count), :] = done[kb]


def one_kernel(one, freq_count, last, table_ref, angle_ref, *refs):
    if last:
        row_ref, in_ref, local_ref, column_ref, out_ref, energy_ref = refs[:6]
        scratch = refs[6:]
    else:
        row_ref, own_ref, got_ref, own_aux, got_aux, out_ref, column_ref = refs[:7]
        scratch = refs[7:]
    e_ref, u_ref, d_ref, n_ref, w_ref, acc_ref, c_ref, known_ref = scratch
    known_ref[...] = table_ref[...]
    blocks = freq_count // ROWS
    lane = lanes()
    for ref in (e_ref, u_ref, d_ref):
        clear(ref, one.slabs, freq_count)
    aux_at = pl.ds(one.slabs * freq_count, ROWS)
    owner = jnp.broadcast_to(row_ref[1:2, :], (ROWS, LANES)) > 0.5
    if last:
        aux = in_ref[aux_at, :]
        up = lane < 0
        for j in range(one.dir_count):
            if sine_up(j, one.dir_count):
                up = up | (lane == column_lane(one, j))
    else:
        aux = jnp.where(owner, own_aux[pl.ds(0, ROWS), :], got_aux[pl.ds(0, ROWS), :])
        out_ref[aux_at, :] = aux
    mask = every_row(aux, 3)
    set_wind(one, freq_count, table_ref, angle_ref, aux, w_ref)
    for kb in range(blocks):
        at = pl.ds(kb * ROWS, ROWS)
        total = jnp.zeros((ROWS, LANES), jnp.float32)
        if last:
            speed = table_ref[0, at, :]
            beyond = jnp.where(up == owner, local_ref[at, :], column_ref[at, :])
        done = []
        if last:
            state = [in_ref[slab_at(r, kb, freq_count), :] for r in range(one.slabs)]
            below = [turn(value, 1) for value in state]
            above = [turn(value, -1) for value in state]
        for r in range(one.slabs):
            if last:
                here = state[r]
                along = jnp.where(angle_ref[1, r] > 0, below[r], above[r])
                for b in range(one.blocks):
                    j = one.direction(b, r)
                    to = b * one.width + (0 if sine_up(j, one.dir_count) else NEAR - 1)
                    along = jnp.where(lane == to, turn(beyond, to - column_lane(one, j)), along)
                start = (
                    here
                    - speed * angle_ref[2, r] * here
                    - speed * angle_ref[3, r] * (here - along)
                ) * (mask * STATE)
            else:
                start = jnp.where(owner, own_ref[slab_at(r, kb, freq_count), :], got_ref[slab_at(r, kb, freq_count), :])
            done.append(start)
            total = total + start
        for r, start in enumerate(done):
            e_ref[r, pl.ds(PAD + kb * ROWS, ROWS), :] = start
        acc_ref[at, :] = total

    @pl.when(jnp.max(aux[3:4]) > 0.5)
    def _():
        sub_steps(one, freq_count, known_ref, e_ref, u_ref, d_ref, n_ref, w_ref, acc_ref, c_ref)

    store_state(one, freq_count, e_ref, mask * (1.0 / STATE), out_ref)
    if last:
        energy = jnp.sum(acc_ref[...], axis=0, keepdims=True) * (mask[0:1] * (1.0 / (STATE * freq_count * one.dir_count)))
        energy_ref[...] = jnp.concatenate(
            [energy, aux[2:3] - 1.0, jnp.zeros((ROWS - 2, LANES), jnp.float32)], axis=0
        )
    else:
        for kb in range(blocks):
            column_ref[pl.ds(kb * ROWS, ROWS), :] = take_column(
                one, one, NEAR_ENDS, lambda r: out_ref[slab_at(r, kb, freq_count), :], lane
            )


def two_kernel(one, two, freq_count, slot_count, last, code_ref, table_ref, angle_ref, row_ref, *refs):
    if last:
        in_ref, pair_ref, cross_ref, local_ref, other_ref, out_ref, energy_ref = refs[:7]
        scratch = refs[7:]
    else:
        own_ref, got_ref, own_aux, got_aux, cross_ref, out_ref, column_ref, pair_out, cross_out = refs[:9]
        scratch = refs[9:]
    e_ref, u_ref, d_ref, n_ref, w_ref, acc_ref, c_ref, known_ref = scratch
    known_ref[...] = table_ref[...]
    blocks = freq_count // ROWS
    lane = lanes()
    slot = lane % two.width
    for ref in (e_ref, u_ref, d_ref):
        clear(ref, two.slabs, freq_count)
    aux_at = pl.ds(two.slabs * freq_count, ROWS)
    parity = code_ref[0] % 2
    inner = (code_ref[0] < 2).astype(jnp.float32)
    owner = jnp.broadcast_to(row_ref[1:2, :], (ROWS, LANES)) > 0.5
    from_cross = flow_mask(lane, two.width, 1 - parity)
    from_pair = flow_mask(lane, two.width, parity)
    if last:
        aux = in_ref[aux_at, :]
        mask = every_row(aux, 3)
    else:
        second = pl.ds(ROWS, ROWS)
        aux = own_aux[second, :] + got_aux[second, :]
        out_ref[aux_at, :] = aux
        mask, got_mask = every_row(own_aux[second, :], 3), every_row(got_aux[second, :], 3)
    set_wind(two, freq_count, table_ref, angle_ref, aux, w_ref)
    for kb in range(blocks):
        at = pl.ds(kb * ROWS, ROWS)
        speed = table_ref[0, at, :]
        total = jnp.zeros((ROWS, LANES), jnp.float32)
        done = []
        slabs = range(two.slabs)
        upward = [angle_ref[1, r] > 0 for r in slabs]
        flow_x = [speed * angle_ref[2, r] for r in slabs]
        flow_y = [speed * angle_ref[3, r] for r in slabs]

        def neighbours(values):
            below = [turn(value, 1) for value in values]
            above = [turn(value, -1) for value in values]
            return [jnp.where(upward[r], below[r], above[r]) for r in slabs]

        here = [(in_ref if last else own_ref)[slab_at(r, kb, freq_count), :] for r in slabs]
        along = neighbours(here)
        across = [loosen(cross_ref, r * blocks + kb) * inner for r in slabs]
        if last:
            beside = [loosen(pair_ref, r * blocks + kb) for r in slabs]
        else:
            beside = [got_ref[slab_at(r, kb, freq_count), :] for r in slabs]
        for r in slabs:
            nearby = jnp.where(from_cross, across[r], jnp.where(from_pair, beside[r], 0.0))
            if last:
                beyond = local_ref[at, :]
                for b in range(two.blocks):
                    j = two.direction(b, r)
                    start = b * two.width
                    if sine_up(j, two.dir_count):
                        to = start + COAST
                        along[r] = jnp.where((lane == to) & ~owner, turn(beyond, to - column_lane(one, j)), along[r])
                    else:
                        to = start + COAST + REST - 1
                        along[r] = jnp.where((lane == to) & owner, turn(beyond, to - column_lane(one, j)), along[r])
                        along[r] = jnp.where((lane == start + COAST - 1) & ~owner, 0.0, along[r])
            else:
                along[r] = jnp.where((slot == 0) & upward[r], 0.0, along[r])
            done.append(
                (here[r] - flow_x[r] * (here[r] - nearby) - flow_y[r] * (here[r] - along[r])) * (mask * STATE)
            )
        if not last:
            here = [turn(beside[r], COAST + REST) for r in slabs]
            along = neighbours(here)
            for r in slabs:
                nearby = jnp.where((slot == COAST + REST - 1) & ~upward[r], 0.0, along[r])
                done[r] = done[r] + (
                    here[r] - flow_x[r] * here[r] - flow_y[r] * (here[r] - nearby)
                ) * (got_mask * STATE)
        for r in slabs:
            total = total + done[r]
        for r, start in enumerate(done):
            e_ref[r, pl.ds(PAD + kb * ROWS, ROWS), :] = start
        acc_ref[at, :] = total
    if last:
        cards = energy_ref.shape[0]
        card = lax.broadcasted_iota(jnp.int32, (cards, LANES), 0) * slot_count
        place = lax.broadcasted_iota(jnp.int32, (LANES, LANES), 0)

        def to_cards(energy, deal):
            deal = deal.astype(jnp.int32)
            to_card = jnp.where((deal >= card) & (deal < card + slot_count), energy, 0.0)
            to_slot = (lax.rem(jnp.maximum(deal, 0), slot_count) == place).astype(jnp.float32)
            return lax.dot_general(
                to_card, to_slot, (((1,), (1,)), ((), ())),
                precision=lax.Precision.HIGHEST, preferred_element_type=jnp.float32,
            )

        elsewhere = to_cards(other_ref[0:1], other_ref[1:2])
    sub_steps(two, freq_count, known_ref, e_ref, u_ref, d_ref, n_ref, w_ref, acc_ref, c_ref)
    scale = every_row(aux, 3) * (1.0 / STATE)
    store_state(two, freq_count, e_ref, scale, out_ref)
    if last:
        energy = jnp.sum(acc_ref[...], axis=0, keepdims=True) * (scale[0:1] / (freq_count * two.dir_count))
        energy_ref[...] = elsewhere + to_cards(energy, aux[2:3] - 1.0)
    else:
        for kb in range(blocks):
            column_ref[pl.ds(kb * ROWS, ROWS), :] = take_column(
                one, two, REST_ENDS, lambda r: out_ref[slab_at(r, kb, freq_count), :], lane
            )
        for ref, wanted in ((pair_out, 1 - parity), (cross_out, parity)):
            chosen = flow_mask(lane, two.width, wanted)
            for g, value in enumerate(
                squeeze(lambda i: out_ref[pl.ds(i * ROWS, ROWS), :], two.slabs * blocks, chosen)
            ):
                ref[pl.ds(g * ROWS, ROWS), :] = value


def gather_kernel(
    one, two, freq_count, row_ref, one_ref, one_got, two_ref, two_got, out_hbm, after_ref, out_ref, sems
):
    dir_count = one.dir_count
    chunk = ROWS * dir_count
    lane = lanes()
    mask = every_row(row_ref[...], 0)
    copies = []
    for kb in range(freq_count // ROWS):
        near = [turn(one_got[slab_at(r, kb, freq_count), :], one.width) for r in range(one.slabs)]
        coast = [turn(two_got[slab_at(r, kb, freq_count), :], -(COAST + REST)) for r in range(two.slabs)]
        for some in range(0, dir_count, 12):
            js = range(some, some + 12)
            value, rest = {}, {}
            for j in js:
                b, r = one.find(j)
                start = b * one.width
                mixed = jnp.where(within(lane, start, one.width), one_ref[slab_at(r, kb, freq_count), :], near[r])
                value[j] = turn(mixed, COAST + REST - start)
            for j in js:
                b, r = two.find(j)
                start = b * two.width
                mixed = jnp.where(within(lane, start, COAST + REST), two_ref[slab_at(r, kb, freq_count), :], coast[r])
                rest[j] = turn(mixed, -start)
            for j in js:
                whole = jnp.where(within(lane, COAST + REST, 2 * NEAR), value[j], rest[j]) * mask
                out_ref[pl.ds(kb * chunk + j, ROWS, stride=dir_count), :] = whole
        rows = pl.ds(kb * chunk, chunk)
        copies.append(pltpu.make_async_copy(out_ref.at[rows], out_hbm.at[rows], sems.at[kb]))
        copies[kb].start()
    for copy in copies:
        copy.wait()
    after_ref[...] = row_ref[...]


def energy_kernel(shared_ref, after_ref, energy_ref):
    energy_ref[...] = jnp.sum(shared_ref[...], axis=0, keepdims=True)[:, :energy_ref.shape[1]]


def coast_width(tile_count, cell_count):
    capacity = cell_count // tile_count
    spread = tile_count * (tile_count - 8) // 8
    return -(-spread // (tile_count - 1)) * capacity


def shards(spectrum, sea_mask, card_deal, wind):
    freq_count, dir_count, row_count, row_width = spectrum.shape
    cell_count = row_count * row_width
    tile_count = lax.axis_size("tile")
    slot_count = cell_count // 8
    assert row_count == 1 and cell_count == LANES and coast_width(tile_count, cell_count) <= COAST
    here = lax.axis_index("tile")
    at_end = (here == 0) | (here == tile_count - 1)
    code = (here % 2 + 2 * at_end.astype(jnp.int32)).astype(jnp.int32).reshape(1)
    one, two = Pack(3, NEAR, dir_count, 0), Pack(4, 32, dir_count, 1)
    table = jnp.asarray(tables(freq_count, dir_count))
    one_rows, two_rows = one.slabs * freq_count, two.slabs * freq_count
    squeezed = -(-two_rows // ROWS // len(SQUEEZE)) * ROWS

    def array(*shape):
        return jax.ShapeDtypeStruct(shape, jnp.float32)

    smem = pl.BlockSpec(memory_space=pltpu.SMEM)
    vmem = pl.BlockSpec(memory_space=pltpu.VMEM)
    hbm = pl.BlockSpec(memory_space=pltpu.HBM)

    def params(rows, steps=SUB, vmem=48):
        return dict(
            compiler_params=pltpu.CompilerParams(vmem_limit_bytes=vmem * 1024 * 1024),
            cost_estimate=pl.CostEstimate(
                flops=rows // ROWS * steps * 8_000_000, bytes_accessed=8 * rows * LANES, transcendentals=0
            ),
        )

    def scratch(pack):
        padded = pltpu.VMEM((pack.slabs, freq_count + 2 * PAD, LANES), jnp.float32)
        plain = pltpu.VMEM((pack.slabs, freq_count, LANES), jnp.float32)
        column = pltpu.VMEM((freq_count, LANES), jnp.float32)
        return [padded, padded, padded, plain, plain, column, column, pltpu.VMEM(table.shape, jnp.float32)]

    group_count = lax.axis_size("groups")
    chip_swap = []
    for g in range(group_count):
        for i in range(tile_count):
            other, there = g, (i + 1 if i % 2 else i - 1)
            if not 0 <= there < tile_count:
                other, there = (g ^ 1 if g ^ 1 < group_count else g), i
            chip_swap.append((g * tile_count + i, other * tile_count + there))

    def to_pair(value):
        return lax.ppermute(value, "tile", [(i, i ^ 1) for i in range(tile_count)])

    def to_next(value):
        return lax.ppermute(value, ("groups", "tile"), chip_swap)

    one_angles, two_angles = jnp.asarray(one.rows()), jnp.asarray(two.rows())
    flat = spectrum.reshape(freq_count * dir_count, cell_count)
    whole = pltpu.VMEM((freq_count * dir_count, LANES), jnp.float32)
    chunks = pltpu.SemaphoreType.DMA((freq_count // ROWS,))
    one_own, one_send = pl.pallas_call(
        functools.partial(near_kernel, one, freq_count),
        out_shape=(array(one_rows, LANES), array(one_rows, LANES)),
        in_specs=[vmem],
        out_specs=(vmem,) * 2,
        name="near",
        **params(1440, 1),
    )(flat)
    row, own_aux, send_aux = pl.pallas_call(
        functools.partial(aux_kernel, one, two),
        out_shape=(array(ROWS, LANES), array(2 * ROWS, LANES), array(2 * ROWS, LANES)),
        in_specs=[vmem] * 3,
        out_specs=(vmem,) * 3,
        name="aux",
        **params(80, 1),
    )(sea_mask, wind.reshape(2, cell_count), card_deal)
    one_got = to_pair(one_send)
    got_aux = to_pair(send_aux)
    two_own, two_send, cross = pl.pallas_call(
        functools.partial(coast_kernel, two, freq_count),
        out_shape=(array(two_rows, LANES), array(two_rows, LANES), array(squeezed, LANES)),
        in_specs=[smem, vmem, vmem],
        out_specs=(vmem,) * 3,
        name="coast",
        **params(1440, 1),
    )(code, flat, row)
    cross_got = to_next(cross)
    two_got = to_pair(two_send)
    one_state, one_column = pl.pallas_call(
        functools.partial(one_kernel, one, freq_count, False),
        out_shape=(array(one_rows + ROWS, LANES), array(freq_count, LANES)),
        in_specs=[vmem] * 7,
        out_specs=(vmem,) * 2,
        scratch_shapes=scratch(one),
        name="first_one",
        **params(one_rows),
    )(table, one_angles, row, one_own, one_got, own_aux, got_aux)
    column_got = to_pair(one_column)
    two_state, two_column, pair, cross = pl.pallas_call(
        functools.partial(two_kernel, one, two, freq_count, slot_count, False),
        out_shape=(
            array(two_rows + ROWS, LANES), array(freq_count, LANES), array(squeezed, LANES), array(squeezed, LANES),
        ),
        in_specs=[smem] + [vmem] * 8,
        out_specs=(vmem,) * 4,
        scratch_shapes=scratch(two),
        name="first_two",
        **params(two_rows),
    )(code, table, two_angles, row, two_own, two_got, own_aux, got_aux, cross_got)
    cross_got = to_next(cross)
    pair_got = to_pair(pair)
    one_state, one_energy = pl.pallas_call(
        functools.partial(one_kernel, one, freq_count, True),
        out_shape=(array(one_rows, LANES), array(ROWS, LANES)),
        in_specs=[vmem] * 6,
        out_specs=(vmem,) * 2,
        scratch_shapes=scratch(one),
        name="second_one",
        **params(one_rows),
    )(table, one_angles, row, one_state, two_column, column_got)
    one_got = to_pair(one_state)
    two_state, energy = pl.pallas_call(
        functools.partial(two_kernel, one, two, freq_count, slot_count, True),
        out_shape=(array(two_rows, LANES), array(tile_count, LANES)),
        in_specs=[smem] + [vmem] * 8,
        out_specs=(vmem,) * 2,
        scratch_shapes=scratch(two),
        name="second_two",
        **params(two_rows),
    )(code, table, two_angles, row, two_state, pair_got, cross_got, one_column, one_energy)
    two_got = to_pair(two_state)
    shared = lax.all_to_all(
        energy.reshape(tile_count, 1, LANES), "tile", split_axis=0, concat_axis=0, tiled=True
    )
    out, after = pl.pallas_call(
        functools.partial(gather_kernel, one, two, freq_count),
        out_shape=(array(freq_count * dir_count, LANES), array(ROWS, LANES)),
        in_specs=[vmem] * 5,
        out_specs=(hbm, vmem),
        scratch_shapes=[whole, chunks],
        name="gather",
        **params(1440, 1),
    )(row, one_state, one_got, two_state, two_got)
    card_energy = pl.pallas_call(
        energy_kernel,
        out_shape=array(1, slot_count),
        in_specs=[vmem] * 2,
        out_specs=vmem,
        name="energy",
        **params(80, 1),
    )(shared.reshape(tile_count, LANES), after)
    return out.reshape(freq_count, dir_count, row_count, row_width), card_energy.reshape(slot_count)


def solution(mesh):
    placed = (
        P(None, None, ("groups", "tile"), None),
        P(("groups", "tile"), None),
        P(("groups", "tile"), None),
        P(None, ("groups", "tile"), None),
    )
    return jax.shard_map(
        shards,
        mesh=mesh,
        in_specs=placed,
        out_specs=(P(None, None, ("groups", "tile"), None), P(("groups", "tile"))),
        check_vma=False,
    )
```

profile of v0, /device:TPU:0, one launch (start us, length us, event | category | flops | bytes accessed | tf_op | source)
XLA Modules:
  0.0 35.8 jit_solution(3279875135378915987)
XLA Ops:
  0.6 0.0 copy-start
  0.6 1.1 %copy-done = f32[40,36,1,128]{3,2,1,0:T(1,128)S(1)} copy-done((f32[40,36,1,128]{3,2,1,0:T(1,128)S(1)}, f32[40,36,1,128]{3,2,1,0:T(1,128)}, u32[]{:S(2)}) %copy-start) | copy-done | bytes 737304
  1.7 0.0 copy-start.1
  1.7 1.1 %near.1 = (f32[480,128]{1,0:T(8,128)S(1)}, f32[480,128]{1,0:T(8,128)S(1)}) custom-call(f32[1440,128]{1,0:T(8,128)S(1)} %bitcast.10), custom_call_target="tpu_custom_call" | custom-call | flops 1440000000 | bytes 1474560 | tf_op jit(solution)/shard_map/near/pallas_call | solution.py:769
  2.9 0.0 copy-start.4
  2.9 0.0 copy-start.2
  2.9 0.0 copy-start.3
  2.9 0.5 %collective-permute-start = (f32[480,128]{1,0:T(8,128)S(1)}, f32[480,128]{1,0:T(8,128)S(1)}, u32[]{:S(2)}, u32[]{:S(2)}) collective-permute-start(f32[480,128]{1,0:T(8,128)S(1)} %get-tuple-element.24), channel_id=1, source_target_pairs={{0,1},{1,0},{2,3},{3,2},{4,5},{5,4},{6,7},{7,6},{8,9},{9,8},{10,11... | collective-permute-start | bytes 737288 | tf_op jit(solution)/shard_map/ppermute | solution.py:760
  3.4 0.1 copy-done.4
  3.5 0.0 copy-done.2
  3.6 0.0 copy-done.3
  3.6 0.1 aux.1
  3.7 0.5 %collective-permute-start.1 = (f32[16,128]{1,0:T(8,128)S(1)}, f32[16,128]{1,0:T(8,128)S(1)}, u32[]{:S(2)}, u32[]{:S(2)}) collective-permute-start(f32[16,128]{1,0:T(8,128)S(1)} %get-tuple-element.26), channel_id=1, source_target_pairs={{0,1},{1,0},{2,3},{3,2},{4,5},{5,4},{6,7},{7,6},{8,9},{9,8},{10,11... | collective-permute-start | bytes 24584 | tf_op jit(solution)/shard_map/ppermute | solution.py:760
  4.2 0.0 copy-done.1
  4.2 0.0 copy-start.5
  4.2 0.0 copy-start.7
  4.2 0.3 coast.1
  4.5 2.6 %collective-permute-start.3 = (f32[96,128]{1,0:T(8,128)S(1)}, f32[96,128]{1,0:T(8,128)S(1)}, u32[]{:S(2)}, u32[]{:S(2)}) collective-permute-start(f32[96,128]{1,0:T(8,128)S(1)} %get-tuple-element.30), channel_id=1, source_target_pairs={{0,16},{1,2},{2,1},{3,4},{4,3},{5,6},{6,5},{7,8},{8,7},{9,10},{10,... | collective-permute-start | bytes 147464 | tf_op jit(solution)/shard_map/ppermute | solution.py:763
  7.1 0.1 collective-permute-start.2
  7.2 0.0 collective-permute-done.1.refs_4_.refs_3_
  7.2 0.0 collective-permute-done.refs_2_
  7.2 0.0 copy-done.5
  7.2 0.0 copy-done.7
  7.2 0.0 copy-start.6
  7.3 0.3 first_one.1
  7.5 0.4 %collective-permute-start.4 = (f32[40,128]{1,0:T(8,128)S(1)}, f32[40,128]{1,0:T(8,128)S(1)}, u32[]{:S(2)}, u32[]{:S(2)}) collective-permute-start(f32[40,128]{1,0:T(8,128)S(1)} %get-tuple-element.32.refs_3_), channel_id=1, source_target_pairs={{0,1},{1,0},{2,3},{3,2},{4,5},{5,4},{6,7},{7,6},{8,9},{9,8},{10,11... | collective-permute-start | bytes 61448 | tf_op jit(solution)/shard_map/ppermute | solution.py:760
  8.0 1.2 %collective-permute-done.3.refs_4_ = f32[96,128]{1,0:T(8,128)S(1)} collective-permute-done((f32[96,128]{1,0:T(8,128)S(1)}, f32[96,128]{1,0:T(8,128)S(1)}, u32[]{:S(2)}, u32[]{:S(2)}) %collective-permute-start.3) | collective-permute-done | bytes 49184 | tf_op jit(solution)/shard_map/ppermute | solution.py:763
  9.1 0.0 collective-permute-done.2.refs_1_
  9.2 0.0 copy-done.6
  9.2 3.7 %first_two.1 = (f32[368,128]{1,0:T(8,128)S(1)}, f32[40,128]{1,0:T(8,128)S(1)}, f32[96,128]{1,0:T(8,128)S(1)}, f32[96,128]{1,0:T(8,128)S(1)}) custom-call(s32[1]{0:T(128)} %bitcast.2.code_ref, f32[5,40,128]{2,1,0:T(8,128)S(1)} %copy-done.7, f32[4,9,8,128]{3,2,1,0:T(8,128)S(1)} %copy-done.6, f32[8,128]{1,0:T(8,128)S(1)} %get-tuple-element.22.refs_0_.row_ref, ...), custom_call_target="tpu_custom_call" | custom-call | flops 2880000000 | bytes 368640 | tf_op jit(solution)/shard_map/first_two/pallas_call | solution.py:807
  12.9 0.2 collective-permute-start.6
  13.0 2.0 %collective-permute-start.7 = (f32[96,128]{1,0:T(8,128)S(1)}, f32[96,128]{1,0:T(8,128)S(1)}, u32[]{:S(2)}, u32[]{:S(2)}) collective-permute-start(f32[96,128]{1,0:T(8,128)S(1)} %get-tuple-element.36), channel_id=1, source_target_pairs={{0,16},{1,2},{2,1},{3,4},{4,3},{5,6},{6,5},{7,8},{8,7},{9,10},{10,... | collective-permute-start | bytes 147464 | tf_op jit(solution)/shard_map/ppermute | solution.py:763
  15.1 0.0 collective-permute-done.4.refs_3_
  15.1 0.4 %second_one.1 = (f32[480,128]{1,0:T(8,128)S(1)}, f32[8,128]{1,0:T(8,128)S(1)}) custom-call(f32[5,40,128]{2,1,0:T(8,128)S(1)} %copy-done.7, f32[4,12,8,128]{3,2,1,0:T(8,128)S(1)} %copy-done.5, f32[8,128]{1,0:T(8,128)S(1)} %get-tuple-element.22.refs_0_.row_ref, f32[488,128]{1,0:T(8,128)S(1)} %get-tuple-element.27.refs_1_, ...), custom_call_target="tpu_custom_call" | custom-call | flops 3840000000 | bytes 491520 | tf_op jit(solution)/shard_map/second_one/pallas_call | solution.py:820
  15.4 0.9 %collective-permute-start.5 = (f32[480,128]{1,0:T(8,128)S(1)}, f32[480,128]{1,0:T(8,128)S(1)}, u32[]{:S(2)}, u32[]{:S(2)}) collective-permute-start(f32[480,128]{1,0:T(8,128)S(1)} %get-tuple-element.33.one_ref), channel_id=1, source_target_pairs={{0,1},{1,0},{2,3},{3,2},{4,5},{5,4},{6,7},{7,6},{8,9},{9,8},{10,11... | collective-permute-start | bytes 737288 | tf_op jit(solution)/shard_map/ppermute | solution.py:760
  16.3 0.0 collective-permute-done.6.refs_1_
  16.3 0.8 %collective-permute-done.7.refs_2_ = f32[96,128]{1,0:T(8,128)S(1)} collective-permute-done((f32[96,128]{1,0:T(8,128)S(1)}, f32[96,128]{1,0:T(8,128)S(1)}, u32[]{:S(2)}, u32[]{:S(2)}) %collective-permute-start.7) | collective-permute-done | bytes 49184 | tf_op jit(solution)/shard_map/ppermute | solution.py:763
  17.1 4.1 %second_two.1 = (f32[360,128]{1,0:T(8,128)S(1)}, f32[16,128]{1,0:T(8,128)}) custom-call(s32[1]{0:T(128)} %bitcast.2.code_ref, f32[5,40,128]{2,1,0:T(8,128)S(1)} %copy-done.7, f32[4,9,8,128]{3,2,1,0:T(8,128)S(1)} %copy-done.6, f32[8,128]{1,0:T(8,128)S(1)} %get-tuple-element.22.refs_0_.row_ref, f32[368,128]{1,0:T(8,128)S(1)} %get-tuple-element.34.refs_0_, ...), custom_call_target="tpu_custom_call" | custom-call | flops 2880000000 | bytes 368640 | tf_op jit(solution)/shard_map/second_two/pallas_call | solution.py:830
  21.3 0.5 %collective-permute-start.8 = (f32[360,128]{1,0:T(8,128)S(1)}, f32[360,128]{1,0:T(8,128)S(1)}, u32[]{:S(2)}, u32[]{:S(2)}) collective-permute-start(f32[360,128]{1,0:T(8,128)S(1)} %get-tuple-element.38.two_ref), channel_id=1, source_target_pairs={{0,1},{1,0},{2,3},{3,2},{4,5},{5,4},{6,7},{7,6},{8,9},{9,8},{10,11... | collective-permute-start | bytes 552968 | tf_op jit(solution)/shard_map/ppermute | solution.py:760
  21.8 7.1 %all-to-all-start = ((f32[16,1,128]{2,1,0:T(1,128)}), f32[16,1,128]{2,1,0:T(1,128)S(1)}, u32[]{:S(2)}, u32[]{:S(2)}) async-start(f32[16,1,128]{2,1,0:T(1,128)} %bitcast.5), calls=%async_computation | async-start | bytes 16384 | tf_op jit(solution)/shard_map/all_to_all | solution.py:840
  28.9 0.0 collective-permute-done.8.two_got
  28.9 0.0 collective-permute-done.5.one_got
  28.9 1.5 %gather.1 = (f32[1440,128]{1,0:T(8,128)}, f32[8,128]{1,0:T(8,128)S(1)}) custom-call(f32[8,128]{1,0:T(8,128)S(1)} %get-tuple-element.22.refs_0_.row_ref, f32[480,128]{1,0:T(8,128)S(1)} %get-tuple-element.33.one_ref, f32[480,128]{1,0:T(8,128)S(1)} %collective-permute-done.5.one_got, f32[360,128]{1,0:T(8,128)S(1)} %get-tuple-element.38.two_ref, ...), custom_call_target="tpu_custom_call" | custom-call | flops 1440000000 | bytes 1474560 | tf_op jit(solution)/shard_map/gather/pallas_call | solution.py:843
  30.4 4.9 %all-to-all-done = f32[16,1,128]{2,1,0:T(1,128)S(1)} async-done(((f32[16,1,128]{2,1,0:T(1,128)}), f32[16,1,128]{2,1,0:T(1,128)S(1)}, u32[]{:S(2)}, u32[]{:S(2)}) %all-to-all-start) | async-done | bytes 8224 | tf_op jit(solution)/shard_map/all_to_all | solution.py:840
  35.3 0.5 %energy.1 = f32[1,16]{1,0:T(1,128)} custom-call(f32[16,128]{1,0:T(8,128)S(1)} %bitcast.9, f32[8,128]{1,0:T(8,128)S(1)} %get-tuple-element.41.after_ref), custom_call_target="tpu_custom_call" | custom-call | flops 80000000 | bytes 81920 | tf_op jit(solution)/shard_map/energy/pallas_call | solution.py:852
Async XLA Ops:
  0.6 1.1 %copy-start = (f32[40,36,1,128]{3,2,1,0:T(1,128)S(1)}, f32[40,36,1,128]{3,2,1,0:T(1,128)}, u32[]{:S(2)}) copy-start(f32[40,36,1,128]{3,2,1,0:T(1,128)} %param.7) | copy-start | bytes 2211844
  1.7 2.4 %copy-start.1 = (f32[40,36,1,128]{3,2,1,0:T(1,128)S(1)}, f32[40,36,1,128]{3,2,1,0:T(1,128)}, u32[]{:S(2)}) copy-start(f32[40,36,1,128]{3,2,1,0:T(1,128)} %param.7) | copy-start | bytes 2211844
  2.9 0.7 %copy-start.4 = (s32[1,128]{1,0:T(1,128)S(1)}, s32[1,128]{1,0:T(1,128)}, u32[]{:S(2)}) copy-start(s32[1,128]{1,0:T(1,128)} %deal_ref.1) | copy-start | bytes 1540
  2.9 0.7 %copy-start.2 = (f32[2,1,128]{2,1,0:T(1,128)S(1)}, f32[2,1,128]{2,1,0:T(1,128)}, u32[]{:S(2)}) copy-start(f32[2,1,128]{2,1,0:T(1,128)} %param.10) | copy-start | bytes 3076
  2.9 0.7 %copy-start.3 = (s32[1,128]{1,0:T(1,128)S(1)}, s32[1,128]{1,0:T(1,128)}, u32[]{:S(2)}) copy-start(s32[1,128]{1,0:T(1,128)} %mask_ref.1) | copy-start | bytes 1540
  2.9 4.3 %collective-permute-start = (f32[480,128]{1,0:T(8,128)S(1)}, f32[480,128]{1,0:T(8,128)S(1)}, u32[]{:S(2)}, u32[]{:S(2)}) collective-permute-start(f32[480,128]{1,0:T(8,128)S(1)} %get-tuple-element.24), channel_id=1, source_target_pairs={{0,1},{1,0},{2,3},{3,2},{4,5},{5,4},{6,7},{7,6},{8,9},{9,8},{10,11... | collective-permute-start | bytes 737288 | tf_op jit(solution)/shard_map/ppermute | solution.py:760
  3.7 3.6 %collective-permute-start.1 = (f32[16,128]{1,0:T(8,128)S(1)}, f32[16,128]{1,0:T(8,128)S(1)}, u32[]{:S(2)}, u32[]{:S(2)}) collective-permute-start(f32[16,128]{1,0:T(8,128)S(1)} %get-tuple-element.26), channel_id=1, source_target_pairs={{0,1},{1,0},{2,3},{3,2},{4,5},{5,4},{6,7},{7,6},{8,9},{9,8},{10,11... | collective-permute-start | bytes 24584 | tf_op jit(solution)/shard_map/ppermute | solution.py:760
  4.2 3.0 %copy-start.5 = (f32[4,12,8,128]{3,2,1,0:T(8,128)S(1)}, f32[4,12,8,128]{3,2,1,0:T(8,128)}, u32[]{:S(2)}) copy-start(f32[4,12,8,128]{3,2,1,0:T(8,128)} %constant.28.clone.angle_ref) | copy-start | bytes 589828
  4.2 3.1 %copy-start.7 = (f32[5,40,128]{2,1,0:T(8,128)S(1)}, f32[5,40,128]{2,1,0:T(8,128)}, u32[]{:S(2)}) copy-start(f32[5,40,128]{2,1,0:T(8,128)} %constant.27.clone.table_ref) | copy-start | bytes 307204
  4.5 4.7 %collective-permute-start.3 = (f32[96,128]{1,0:T(8,128)S(1)}, f32[96,128]{1,0:T(8,128)S(1)}, u32[]{:S(2)}, u32[]{:S(2)}) collective-permute-start(f32[96,128]{1,0:T(8,128)S(1)} %get-tuple-element.30), channel_id=1, source_target_pairs={{0,16},{1,2},{2,1},{3,4},{4,3},{5,6},{6,5},{7,8},{8,7},{9,10},{10,... | collective-permute-start | bytes 147464 | tf_op jit(solution)/shard_map/ppermute | solution.py:763
  7.1 2.1 %collective-permute-start.2 = (f32[360,128]{1,0:T(8,128)S(1)}, f32[360,128]{1,0:T(8,128)S(1)}, u32[]{:S(2)}, u32[]{:S(2)}) collective-permute-start(f32[360,128]{1,0:T(8,128)S(1)} %get-tuple-element.29), channel_id=1, source_target_pairs={{0,1},{1,0},{2,3},{3,2},{4,5},{5,4},{6,7},{7,6},{8,9},{9,8},{10,11... | collective-permute-start | bytes 552968 | tf_op jit(solution)/shard_map/ppermute | solution.py:760
  7.2 1.9 %copy-start.6 = (f32[4,9,8,128]{3,2,1,0:T(8,128)S(1)}, f32[4,9,8,128]{3,2,1,0:T(8,128)}, u32[]{:S(2)}) copy-start(f32[4,9,8,128]{3,2,1,0:T(8,128)} %constant.29.clone.angle_ref) | copy-start | bytes 442372
  7.5 7.5 %collective-permute-start.4 = (f32[40,128]{1,0:T(8,128)S(1)}, f32[40,128]{1,0:T(8,128)S(1)}, u32[]{:S(2)}, u32[]{:S(2)}) collective-permute-start(f32[40,128]{1,0:T(8,128)S(1)} %get-tuple-element.32.refs_3_), channel_id=1, source_target_pairs={{0,1},{1,0},{2,3},{3,2},{4,5},{5,4},{6,7},{7,6},{8,9},{9,8},{10,11... | collective-permute-start | bytes 61448 | tf_op jit(solution)/shard_map/ppermute | solution.py:760
  12.9 3.5 %collective-permute-start.6 = (f32[96,128]{1,0:T(8,128)S(1)}, f32[96,128]{1,0:T(8,128)S(1)}, u32[]{:S(2)}, u32[]{:S(2)}) collective-permute-start(f32[96,128]{1,0:T(8,128)S(1)} %get-tuple-element.35), channel_id=1, source_target_pairs={{0,1},{1,0},{2,3},{3,2},{4,5},{5,4},{6,7},{7,6},{8,9},{9,8},{10,11... | collective-permute-start | bytes 147464 | tf_op jit(solution)/shard_map/ppermute | solution.py:760
  13.0 4.1 %collective-permute-start.7 = (f32[96,128]{1,0:T(8,128)S(1)}, f32[96,128]{1,0:T(8,128)S(1)}, u32[]{:S(2)}, u32[]{:S(2)}) collective-permute-start(f32[96,128]{1,0:T(8,128)S(1)} %get-tuple-element.36), channel_id=1, source_target_pairs={{0,16},{1,2},{2,1},{3,4},{4,3},{5,6},{6,5},{7,8},{8,7},{9,10},{10,... | collective-permute-start | bytes 147464 | tf_op jit(solution)/shard_map/ppermute | solution.py:763
  15.4 13.5 %collective-permute-start.5 = (f32[480,128]{1,0:T(8,128)S(1)}, f32[480,128]{1,0:T(8,128)S(1)}, u32[]{:S(2)}, u32[]{:S(2)}) collective-permute-start(f32[480,128]{1,0:T(8,128)S(1)} %get-tuple-element.33.one_ref), channel_id=1, source_target_pairs={{0,1},{1,0},{2,3},{3,2},{4,5},{5,4},{6,7},{7,6},{8,9},{9,8},{10,11... | collective-permute-start | bytes 737288 | tf_op jit(solution)/shard_map/ppermute | solution.py:760
  21.3 7.6 %collective-permute-start.8 = (f32[360,128]{1,0:T(8,128)S(1)}, f32[360,128]{1,0:T(8,128)S(1)}, u32[]{:S(2)}, u32[]{:S(2)}) collective-permute-start(f32[360,128]{1,0:T(8,128)S(1)} %get-tuple-element.38.two_ref), channel_id=1, source_target_pairs={{0,1},{1,0},{2,3},{3,2},{4,5},{5,4},{6,7},{7,6},{8,9},{9,8},{10,11... | collective-permute-start | bytes 552968 | tf_op jit(solution)/shard_map/ppermute | solution.py:760
  21.8 13.5 %all-to-all-start = ((f32[16,1,128]{2,1,0:T(1,128)}), f32[16,1,128]{2,1,0:T(1,128)S(1)}, u32[]{:S(2)}, u32[]{:S(2)}) async-start(f32[16,1,128]{2,1,0:T(1,128)} %bitcast.5), calls=%async_computation | async-start | bytes 16384 | tf_op jit(solution)/shard_map/all_to_all | solution.py:840
where the time goes:
time: 35.5 us; the launch traced here: 35.8 us
  starting transfers between devices  14.9 us (42%)
  Pallas kernels  11.9 us (34%)
  waiting for transfers between devices  6.92 us (19%)
  local copies, waits for them, and re-layouts  1.29 us (4%)
  between operations  0.75 us (2%)
    pallas_call x2, Pallas kernels, shards(): pl.pallas_call(functools.partial(two_kernel, one, two, freq_count, slot_c...  7.83 us
    all_to_all x1, starting transfers between devices, shards(): lax.all_to_all(energy.reshape(tile_count, 1, LANES), 'tile', split_axis=0...  7.11 us
    all_to_all x1, waiting for transfers between devices, shards(): lax.all_to_all(energy.reshape(tile_count, 1, LANES), 'tile', split_axis=0...  4.9 us
    ppermute x2, starting transfers between devices, to_next(): return lax.ppermute(value, ('groups', 'tile'), chip_swap)  4.63 us
    ppermute x7, starting transfers between devices, to_pair(): return lax.ppermute(value, 'tile', [(i, i ^ 1) for i in range(tile_count)])  3.16 us
    ppermute x2, waiting for transfers between devices, to_next(): return lax.ppermute(value, ('groups', 'tile'), chip_swap)  2 us
    pallas_call x1, Pallas kernels, shards(): pl.pallas_call(functools.partial(gather_kernel, one, two, freq_count), ou...  1.47 us
    unnamed x16, local copies, waits for them, and re-layouts  1.29 us
  transfers between devices with their start and end apart: 10, of which 3 were waited for; matrix products, arithmetic and copies ran while one was open for 0% of the time, Pallas kernels for 29%

commit v1 on v0

--- a/solution.py
+++ b/solution.py
@@ -283,11 +283,11 @@
     lax.fori_loop(0, SUB, sub_step, 0)
 
 
-def slab_at(r, kb, freq_count):
-    return pl.ds(r * freq_count + kb * ROWS, ROWS)
-
-
-SQUEEZE = (0, COAST, 4 * COAST, 5 * COAST)
+def slab_at(r, kb, freq_count, base=0):
+    return pl.ds(base + r * freq_count + kb * ROWS, ROWS)
+
+
+SQUEEZE = (0, COAST)
 
 
 def flow_mask(lane, width, wanted):
@@ -391,33 +391,32 @@
     return total
 
 
-def aux_kernel(one, two, mask_ref, wind_ref, deal_ref, row_ref, own_ref, send_ref):
-    mask = mask_ref[...].astype(jnp.float32)
+def aux_rows(one, two, mask, wind, deal):
     aux = jnp.concatenate(
-        [
-            wind_ref[...] * mask,
-            (deal_ref[...] + 1).astype(jnp.float32) * mask,
-            mask,
-            jnp.zeros((ROWS - 4, LANES), jnp.float32),
-        ],
-        axis=0,
+        [wind * mask, (deal + 1).astype(jnp.float32) * mask, mask, jnp.zeros((ROWS - 4, LANES), jnp.float32)], axis=0
     )
-    row_ref[...] = jnp.concatenate(
-        [mask, jnp.broadcast_to(mask[:, LANES - 1:LANES], (1, LANES)), jnp.zeros((ROWS - 2, LANES), jnp.float32)], axis=0
-    )
-    own_ref[pl.ds(0, ROWS), :] = pack_aux(one, aux, COAST + REST, 0, NEAR)
-    own_ref[pl.ds(ROWS, ROWS), :] = pack_aux(two, aux, 0, 0, COAST + REST)
-    send_ref[pl.ds(0, ROWS), :] = pack_aux(one, aux, FAR, 0, NEAR)
-    send_ref[pl.ds(ROWS, ROWS), :] = pack_aux(two, aux, FAR + NEAR, COAST, REST)
-
-
-def coast_kernel(two, freq_count, code_ref, spec_ref, row_ref, own_ref, send_ref, cross_ref):
+    own = pack_aux(one, aux, COAST + REST, 0, NEAR), pack_aux(two, aux, 0, 0, COAST + REST)
+    sent = pack_aux(one, aux, FAR, 0, NEAR), pack_aux(two, aux, FAR + NEAR, COAST, REST)
+    return jnp.concatenate(own, axis=0), jnp.concatenate(sent, axis=0)
+
+
+def coast_kernel(
+    one, two, freq_count, spec_ref, mask_ref, wind_ref, deal_ref,
+    own_ref, send_ref, cross_ref, row_ref, own_aux,
+):
     dir_count = two.dir_count
     blocks = freq_count // ROWS
     chunk = ROWS * dir_count
     lane = lanes()
     slot = lane % two.width
-    mask = every_row(row_ref[...], 0)
+    mask = mask_ref[...].astype(jnp.float32)
+    row_ref[...] = jnp.concatenate(
+        [mask, jnp.broadcast_to(mask[:, LANES - 1:LANES], (1, LANES)), jnp.zeros((ROWS - 2, LANES), jnp.float32)], axis=0
+    )
+    own, sent = aux_rows(one, two, mask, wind_ref[...], deal_ref[...])
+    own_aux[...] = own
+    send_ref[pl.ds(two.slabs * freq_count, 2 * ROWS), :] = sent
+    mask = every_row(mask, 0)
     for kb in range(blocks):
         done = []
         for r in range(two.slabs):
@@ -435,8 +434,7 @@
             own_ref[slab_at(r, kb, freq_count), :] = own
             send_ref[slab_at(r, kb, freq_count), :] = sent
 
-    chosen = flow_mask(lane, two.width, code_ref[0] % 2)
-    for g, value in enumerate(squeeze(lambda i: own_ref[pl.ds(i * ROWS, ROWS), :], two.slabs * blocks, chosen)):
+    for g, value in enumerate(squeeze(lambda i: own_ref[pl.ds(i * ROWS, ROWS), :], two.slabs * blocks, slot < COAST)):
         cross_ref[pl.ds(g * ROWS, ROWS), :] = value
 
 
@@ -497,7 +495,7 @@
             if sine_up(j, one.dir_count):
                 up = up | (lane == column_lane(one, j))
     else:
-        aux = jnp.where(owner, own_aux[pl.ds(0, ROWS), :], got_aux[pl.ds(0, ROWS), :])
+        aux = jnp.where(owner, own_aux[pl.ds(0, ROWS), :], got_aux[pl.ds(got_aux.shape[0] - 2 * ROWS, ROWS), :])
         out_ref[aux_at, :] = aux
     mask = every_row(aux, 3)
     set_wind(one, freq_count, table_ref, angle_ref, aux, w_ref)
@@ -552,11 +550,11 @@
 
 def two_kernel(one, two, freq_count, slot_count, last, code_ref, table_ref, angle_ref, row_ref, *refs):
     if last:
-        in_ref, pair_ref, cross_ref, local_ref, other_ref, out_ref, energy_ref = refs[:7]
+        in_ref, pair_ref, cross_ref, local_ref, other_ref, one_ref, out_ref, energy_ref = refs[:8]
+        scratch = refs[8:]
+    else:
+        own_ref, got_ref, own_aux, cross_ref, out_ref, column_ref, coast_out = refs[:7]
         scratch = refs[7:]
-    else:
-        own_ref, got_ref, own_aux, got_aux, cross_ref, out_ref, column_ref, pair_out, cross_out = refs[:9]
-        scratch = refs[9:]
     e_ref, u_ref, d_ref, n_ref, w_ref, acc_ref, c_ref, known_ref = scratch
     known_ref[...] = table_ref[...]
     blocks = freq_count // ROWS
@@ -574,10 +572,10 @@
         aux = in_ref[aux_at, :]
         mask = every_row(aux, 3)
     else:
-        second = pl.ds(ROWS, ROWS)
-        aux = own_aux[second, :] + got_aux[second, :]
+        own_rows, got_rows = own_aux[pl.ds(ROWS, ROWS), :], got_ref[pl.ds(got_ref.shape[0] - ROWS, ROWS), :]
+        aux = own_rows + got_rows
         out_ref[aux_at, :] = aux
-        mask, got_mask = every_row(own_aux[second, :], 3), every_row(got_aux[second, :], 3)
+        mask, got_mask = every_row(own_rows, 3), every_row(got_rows, 3)
     set_wind(two, freq_count, table_ref, angle_ref, aux, w_ref)
     for kb in range(blocks):
         at = pl.ds(kb * ROWS, ROWS)
@@ -647,6 +645,7 @@
                 precision=lax.Precision.HIGHEST, preferred_element_type=jnp.float32,
             )
 
+        out_ref[pl.ds(two.slabs * freq_count, one.slabs * freq_count), :] = one_ref[...]
         elsewhere = to_cards(other_ref[0:1], other_ref[1:2])
     sub_steps(two, freq_count, known_ref, e_ref, u_ref, d_ref, n_ref, w_ref, acc_ref, c_ref)
     scale = every_row(aux, 3) * (1.0 / STATE)
@@ -659,24 +658,22 @@
             column_ref[pl.ds(kb * ROWS, ROWS), :] = take_column(
                 one, two, REST_ENDS, lambda r: out_ref[slab_at(r, kb, freq_count), :], lane
             )
-        for ref, wanted in ((pair_out, 1 - parity), (cross_out, parity)):
-            chosen = flow_mask(lane, two.width, wanted)
-            for g, value in enumerate(
-                squeeze(lambda i: out_ref[pl.ds(i * ROWS, ROWS), :], two.slabs * blocks, chosen)
-            ):
-                ref[pl.ds(g * ROWS, ROWS), :] = value
+        fetch = lambda i: out_ref[pl.ds(i * ROWS, ROWS), :]
+        for g, value in enumerate(squeeze(fetch, two.slabs * blocks, slot < COAST)):
+            coast_out[pl.ds(g * ROWS, ROWS), :] = value
 
 
 def gather_kernel(
-    one, two, freq_count, row_ref, one_ref, one_got, two_ref, two_got, out_hbm, after_ref, out_ref, sems
+    one, two, freq_count, row_ref, two_ref, two_got, out_hbm, after_ref, out_ref, sems
 ):
     dir_count = one.dir_count
     chunk = ROWS * dir_count
     lane = lanes()
     mask = every_row(row_ref[...], 0)
+    base = two.slabs * freq_count
     copies = []
     for kb in range(freq_count // ROWS):
-        near = [turn(one_got[slab_at(r, kb, freq_count), :], one.width) for r in range(one.slabs)]
+        near = [turn(two_got[slab_at(r, kb, freq_count, base), :], one.width) for r in range(one.slabs)]
         coast = [turn(two_got[slab_at(r, kb, freq_count), :], -(COAST + REST)) for r in range(two.slabs)]
         for some in range(0, dir_count, 12):
             js = range(some, some + 12)
@@ -684,7 +681,7 @@
             for j in js:
                 b, r = one.find(j)
                 start = b * one.width
-                mixed = jnp.where(within(lane, start, one.width), one_ref[slab_at(r, kb, freq_count), :], near[r])
+                mixed = jnp.where(within(lane, start, one.width), two_ref[slab_at(r, kb, freq_count, base), :], near[r])
                 value[j] = turn(mixed, COAST + REST - start)
             for j in js:
                 b, r = two.find(j)
@@ -774,26 +771,20 @@
         name="near",
         **params(1440, 1),
     )(flat)
-    row, own_aux, send_aux = pl.pallas_call(
-        functools.partial(aux_kernel, one, two),
-        out_shape=(array(ROWS, LANES), array(2 * ROWS, LANES), array(2 * ROWS, LANES)),
-        in_specs=[vmem] * 3,
-        out_specs=(vmem,) * 3,
-        name="aux",
-        **params(80, 1),
-    )(sea_mask, wind.reshape(2, cell_count), card_deal)
     one_got = to_pair(one_send)
-    got_aux = to_pair(send_aux)
-    two_own, two_send, cross = pl.pallas_call(
-        functools.partial(coast_kernel, two, freq_count),
-        out_shape=(array(two_rows, LANES), array(two_rows, LANES), array(squeezed, LANES)),
-        in_specs=[smem, vmem, vmem],
-        out_specs=(vmem,) * 3,
+    two_own, two_send, cross, row, own_aux = pl.pallas_call(
+        functools.partial(coast_kernel, one, two, freq_count),
+        out_shape=(
+            array(two_rows, LANES), array(two_rows + 2 * ROWS, LANES), array(squeezed, LANES),
+            array(ROWS, LANES), array(2 * ROWS, LANES),
+        ),
+        in_specs=[vmem] * 4,
+        out_specs=(vmem,) * 5,
         name="coast",
         **params(1440, 1),
-    )(code, flat, row)
+    )(flat, sea_mask, wind.reshape(2, cell_count), card_deal)
+    two_got = to_pair(two_send)
     cross_got = to_next(cross)
-    two_got = to_pair(two_send)
     one_state, one_column = pl.pallas_call(
         functools.partial(one_kernel, one, freq_count, False),
         out_shape=(array(one_rows + ROWS, LANES), array(freq_count, LANES)),
@@ -802,21 +793,21 @@
         scratch_shapes=scratch(one),
         name="first_one",
         **params(one_rows),
-    )(table, one_angles, row, one_own, one_got, own_aux, got_aux)
+    )(table, one_angles, row, one_own, one_got, own_aux, two_got)
     column_got = to_pair(one_column)
-    two_state, two_column, pair, cross = pl.pallas_call(
+    two_state, two_column, coast = pl.pallas_call(
         functools.partial(two_kernel, one, two, freq_count, slot_count, False),
         out_shape=(
-            array(two_rows + ROWS, LANES), array(freq_count, LANES), array(squeezed, LANES), array(squeezed, LANES),
+            array(two_rows + ROWS, LANES), array(freq_count, LANES), array(squeezed, LANES),
         ),
-        in_specs=[smem] + [vmem] * 8,
-        out_specs=(vmem,) * 4,
+        in_specs=[smem] + [vmem] * 7,
+        out_specs=(vmem,) * 3,
         scratch_shapes=scratch(two),
         name="first_two",
         **params(two_rows),
-    )(code, table, two_angles, row, two_own, two_got, own_aux, got_aux, cross_got)
-    cross_got = to_next(cross)
-    pair_got = to_pair(pair)
+    )(code, table, two_angles, row, two_own, two_got, own_aux, cross_got)
+    cross_got = to_next(coast)
+    pair_got = to_pair(coast)
     one_state, one_energy = pl.pallas_call(
         functools.partial(one_kernel, one, freq_count, True),
         out_shape=(array(one_rows, LANES), array(ROWS, LANES)),
@@ -826,16 +817,15 @@
         name="second_one",
         **params(one_rows),
     )(table, one_angles, row, one_state, two_column, column_got)
-    one_got = to_pair(one_state)
     two_state, energy = pl.pallas_call(
         functools.partial(two_kernel, one, two, freq_count, slot_count, True),
-        out_shape=(array(two_rows, LANES), array(tile_count, LANES)),
-        in_specs=[smem] + [vmem] * 8,
+        out_shape=(array(two_rows + one_rows, LANES), array(tile_count, LANES)),
+        in_specs=[smem] + [vmem] * 9,
         out_specs=(vmem,) * 2,
         scratch_shapes=scratch(two),
         name="second_two",
         **params(two_rows),
-    )(code, table, two_angles, row, two_state, pair_got, cross_got, one_column, one_energy)
+    )(code, table, two_angles, row, two_state, pair_got, cross_got, one_column, one_energy, one_state)
     two_got = to_pair(two_state)
     shared = lax.all_to_all(
         energy.reshape(tile_count, 1, LANES), "tile", split_axis=0, concat_axis=0, tiled=True
@@ -843,12 +833,12 @@
     out, after = pl.pallas_call(
         functools.partial(gather_kernel, one, two, freq_count),
         out_shape=(array(freq_count * dir_count, LANES), array(ROWS, LANES)),
-        in_specs=[vmem] * 5,
+        in_specs=[vmem] * 3,
         out_specs=(hbm, vmem),
         scratch_shapes=[whole, chunks],
         name="gather",
         **params(1440, 1),
-    )(row, one_state, one_got, two_state, two_got)
+    )(row, two_state, two_got)
     card_energy = pl.pallas_call(
         energy_kernel,
         out_shape=array(1, slot_count),

time: 35.5 us -> 36.6 us (1.031)
  waiting for transfers between devices: 6.92 us -> 9.13 us
  starting transfers between devices: 14.9 us -> 14.1 us
    ppermute x2, waiting for transfers between devices: 2 us -> 4.2 us  [to_next(): return lax.ppermute(value, ('groups', 'tile'), chip_swap)]
    ppermute x7 -> x5, starting transfers between devices: 3.16 us -> 1.25 us  [to_pair(): return lax.ppermute(value, 'tile', [(i, i ^ 1) for i in range(tile_count)])]
    all_to_all x1, starting transfers between devices: 7.11 us -> 8.25 us  [shards(): lax.all_to_all(energy.reshape(tile_count, 1, LANES), 'tile', split_axis=0...]
    unnamed x16 -> x14, local copies, waits for them, and re-layouts: 1.29 us -> 1.29 us
  transfers between devices with their start and end apart: 10 -> 8, of which waited for: 3 -> 3; matrix products, arithmetic and copies ran while one was open for 0% -> 0% of each run, Pallas kernels for 29% -> 16%
where the time goes in v1:
time: 36.6 us; the launch traced here: 37.1 us
  starting transfers between devices  14.1 us (39%)
  Pallas kernels  11.8 us (32%)
  waiting for transfers between devices  9.13 us (25%)
  local copies, waits for them, and re-layouts  1.29 us (4%)
  between operations  0.73 us (2%)
    all_to_all x1, starting transfers between devices, shards(): lax.all_to_all(energy.reshape(tile_count, 1, LANES), 'tile', split_axis=0...  8.25 us
    pallas_call x2, Pallas kernels, shards(): pl.pallas_call(functools.partial(two_kernel, one, two, freq_count, slot_c...  7.76 us
    all_to_all x1, waiting for transfers between devices, shards(): lax.all_to_all(energy.reshape(tile_count, 1, LANES), 'tile', split_axis=0...  4.92 us
    ppermute x2, starting transfers between devices, to_next(): return lax.ppermute(value, ('groups', 'tile'), chip_swap)  4.65 us
    ppermute x2, waiting for transfers between devices, to_next(): return lax.ppermute(value, ('groups', 'tile'), chip_swap)  4.2 us
    pallas_call x1, Pallas kernels, shards(): pl.pallas_call(functools.partial(gather_kernel, one, two, freq_count), ou...  1.47 us
    unnamed x14, local copies, waits for them, and re-layouts  1.29 us
    ppermute x5, starting transfers between devices, to_pair(): return lax.ppermute(value, 'tile', [(i, i ^ 1) for i in range(tile_count)])  1.25 us
  transfers between devices with their start and end apart: 8, of which 3 were waited for; matrix products, arithmetic and copies ran while one was open for 0% of the time, Pallas kernels for 16%

profile of v1, /device:TPU:0, one launch (start us, length us, event | category | flops | bytes accessed | tf_op | source)
XLA Modules:
  0.0 37.1 jit_solution(16191961954199674265)
XLA Ops:
  0.6 0.0 copy-start
  0.6 1.1 %copy-done = f32[40,36,1,128]{3,2,1,0:T(1,128)S(1)} copy-done((f32[40,36,1,128]{3,2,1,0:T(1,128)S(1)}, f32[40,36,1,128]{3,2,1,0:T(1,128)}, u32[]{:S(2)}) %copy-start) | copy-done | bytes 737304
  1.7 1.1 %near.1 = (f32[480,128]{1,0:T(8,128)S(1)}, f32[480,128]{1,0:T(8,128)S(1)}) custom-call(f32[1440,128]{1,0:T(8,128)S(1)} %bitcast.10), custom_call_target="tpu_custom_call" | custom-call | flops 1440000000 | bytes 1474560 | tf_op jit(solution)/shard_map/near/pallas_call | solution.py:766
  2.9 0.0 copy-start.3
  2.9 0.0 copy-start.1
  2.9 0.0 copy-start.2
  2.9 0.5 %collective-permute-start.4 = (f32[480,128]{1,0:T(8,128)S(1)}, f32[480,128]{1,0:T(8,128)S(1)}, u32[]{:S(2)}, u32[]{:S(2)}) collective-permute-start(f32[480,128]{1,0:T(8,128)S(1)} %get-tuple-element.28), channel_id=1, source_target_pairs={{0,1},{1,0},{2,3},{3,2},{4,5},{5,4},{6,7},{7,6},{8,9},{9,8},{10,11... | collective-permute-start | bytes 737288 | tf_op jit(solution)/shard_map/ppermute | solution.py:757
  3.4 0.1 copy-done.3
  3.5 0.0 copy-done.1
  3.6 0.0 copy-done.2
  3.6 0.0 copy-start.4
  3.6 0.0 copy-start.6
  3.6 0.3 coast.1
  3.9 0.5 %collective-permute-start = (f32[376,128]{1,0:T(8,128)S(1)}, f32[376,128]{1,0:T(8,128)S(1)}, u32[]{:S(2)}, u32[]{:S(2)}) collective-permute-start(f32[376,128]{1,0:T(8,128)S(1)} %get-tuple-element.22), channel_id=1, source_target_pairs={{0,1},{1,0},{2,3},{3,2},{4,5},{5,4},{6,7},{7,6},{8,9},{9,8},{10,11... | collective-permute-start | bytes 577544 | tf_op jit(solution)/shard_map/ppermute | solution.py:757
  4.4 2.6 %collective-permute-start.1 = (f32[184,128]{1,0:T(8,128)S(1)}, f32[184,128]{1,0:T(8,128)S(1)}, u32[]{:S(2)}, u32[]{:S(2)}) collective-permute-start(f32[184,128]{1,0:T(8,128)S(1)} %get-tuple-element.24), channel_id=1, source_target_pairs={{0,16},{1,2},{2,1},{3,4},{4,3},{5,6},{6,5},{7,8},{8,7},{9,10},{10,... | collective-permute-start | bytes 282632 | tf_op jit(solution)/shard_map/ppermute | solution.py:760
  6.9 0.0 collective-permute-done.refs_1_.refs_4_
  6.9 0.0 collective-permute-done.4.refs_2_
  7.0 0.0 copy-done.4
  7.0 0.0 copy-done.6
  7.0 0.0 copy-start.5
  7.0 0.3 first_one.1
  7.2 0.2 collective-permute-start.5
  7.5 2.0 %collective-permute-done.1.refs_3_ = f32[184,128]{1,0:T(8,128)S(1)} collective-permute-done((f32[184,128]{1,0:T(8,128)S(1)}, f32[184,128]{1,0:T(8,128)S(1)}, u32[]{:S(2)}, u32[]{:S(2)}) %collective-permute-start.1) | collective-permute-done | bytes 94240 | tf_op jit(solution)/shard_map/ppermute | solution.py:760
  9.5 0.0 copy-done.5
  9.5 3.7 %first_two.1 = (f32[368,128]{1,0:T(8,128)S(1)}, f32[40,128]{1,0:T(8,128)S(1)}, f32[184,128]{1,0:T(8,128)S(1)}) custom-call(s32[1]{0:T(128)} %bitcast.2.code_ref, f32[5,40,128]{2,1,0:T(8,128)S(1)} %copy-done.6, f32[4,9,8,128]{3,2,1,0:T(8,128)S(1)} %copy-done.5, f32[8,128]{1,0:T(8,128)S(1)} %get-tuple-element.20.row_ref.refs_0_, ...), custom_call_target="tpu_custom_call" | custom-call | flops 2880000000 | bytes 368640 | tf_op jit(solution)/shard_map/first_two/pallas_call | solution.py:798
  13.2 2.1 %collective-permute-start.3 = (f32[184,128]{1,0:T(8,128)S(1)}, f32[184,128]{1,0:T(8,128)S(1)}, u32[]{:S(2)}, u32[]{:S(2)}) collective-permute-start(f32[184,128]{1,0:T(8,128)S(1)} %get-tuple-element.26), channel_id=1, source_target_pairs={{0,16},{1,2},{2,1},{3,4},{4,3},{5,6},{6,5},{7,8},{8,7},{9,10},{10,... | collective-permute-start | bytes 282632 | tf_op jit(solution)/shard_map/ppermute | solution.py:760
  15.2 0.0 collective-permute-start.2
  15.2 0.0 collective-permute-done.5.refs_3_
  15.2 0.4 %second_one.1 = (f32[480,128]{1,0:T(8,128)S(1)}, f32[8,128]{1,0:T(8,128)S(1)}) custom-call(f32[5,40,128]{2,1,0:T(8,128)S(1)} %copy-done.6, f32[4,12,8,128]{3,2,1,0:T(8,128)S(1)} %copy-done.4, f32[8,128]{1,0:T(8,128)S(1)} %get-tuple-element.20.row_ref.refs_0_, f32[488,128]{1,0:T(8,128)S(1)} %get-tuple-element.30.refs_1_, ...), custom_call_target="tpu_custom_call" | custom-call | flops 3840000000 | bytes 491520 | tf_op jit(solution)/shard_map/second_one/pallas_call | solution.py:811
  15.6 2.2 %collective-permute-done.3.refs_2_ = f32[184,128]{1,0:T(8,128)S(1)} collective-permute-done((f32[184,128]{1,0:T(8,128)S(1)}, f32[184,128]{1,0:T(8,128)S(1)}, u32[]{:S(2)}, u32[]{:S(2)}) %collective-permute-start.3) | collective-permute-done | bytes 94240 | tf_op jit(solution)/shard_map/ppermute | solution.py:760
  17.8 0.0 collective-permute-done.2.refs_1_
  17.8 4.1 %second_two.1 = (f32[840,128]{1,0:T(8,128)S(1)}, f32[16,128]{1,0:T(8,128)}) custom-call(s32[1]{0:T(128)} %bitcast.2.code_ref, f32[5,40,128]{2,1,0:T(8,128)S(1)} %copy-done.6, f32[4,9,8,128]{3,2,1,0:T(8,128)S(1)} %copy-done.5, f32[8,128]{1,0:T(8,128)S(1)} %get-tuple-element.20.row_ref.refs_0_, f32[368,128]{1,0:T(8,128)S(1)} %get-tuple-element.25.refs_0_, ...), custom_call_target="tpu_custom_call" | custom-call | flops 2880000000 | bytes 368640 | tf_op jit(solution)/shard_map/second_two/pallas_call | solution.py:820
  21.9 0.0 collective-permute-start.6
  21.9 8.3 %all-to-all-start = ((f32[16,1,128]{2,1,0:T(1,128)}), f32[16,1,128]{2,1,0:T(1,128)S(1)}, u32[]{:S(2)}, u32[]{:S(2)}) async-start(f32[16,1,128]{2,1,0:T(1,128)} %bitcast.5), calls=%async_computation | async-start | bytes 16384 | tf_op jit(solution)/shard_map/all_to_all | solution.py:830
  30.2 0.0 collective-permute-done.6.two_got
  30.2 1.5 %gather.1 = (f32[1440,128]{1,0:T(8,128)}, f32[8,128]{1,0:T(8,128)S(1)}) custom-call(f32[8,128]{1,0:T(8,128)S(1)} %get-tuple-element.20.row_ref.refs_0_, f32[840,128]{1,0:T(8,128)S(1)} %get-tuple-element.34.two_ref, f32[840,128]{1,0:T(8,128)S(1)} %collective-permute-done.6.two_got), custom_call_target="tpu_custom_call" | custom-call | flops 1440000000 | bytes 1474560 | tf_op jit(solution)/shard_map/gather/pallas_call | solution.py:833
  31.7 4.9 %all-to-all-done = f32[16,1,128]{2,1,0:T(1,128)S(1)} async-done(((f32[16,1,128]{2,1,0:T(1,128)}), f32[16,1,128]{2,1,0:T(1,128)S(1)}, u32[]{:S(2)}, u32[]{:S(2)}) %all-to-all-start) | async-done | bytes 8224 | tf_op jit(solution)/shard_map/all_to_all | solution.py:830
  36.6 0.5 %energy.1 = f32[1,16]{1,0:T(1,128)} custom-call(f32[16,128]{1,0:T(8,128)S(1)} %bitcast.9, f32[8,128]{1,0:T(8,128)S(1)} %get-tuple-element.37.after_ref), custom_call_target="tpu_custom_call" | custom-call | flops 80000000 | bytes 81920 | tf_op jit(solution)/shard_map/energy/pallas_call | solution.py:842
Async XLA Ops:
  0.6 1.1 %copy-start = (f32[40,36,1,128]{3,2,1,0:T(1,128)S(1)}, f32[40,36,1,128]{3,2,1,0:T(1,128)}, u32[]{:S(2)}) copy-start(f32[40,36,1,128]{3,2,1,0:T(1,128)} %param.7) | copy-start | bytes 2211844
  2.9 0.7 %copy-start.3 = (s32[1,128]{1,0:T(1,128)S(1)}, s32[1,128]{1,0:T(1,128)}, u32[]{:S(2)}) copy-start(s32[1,128]{1,0:T(1,128)} %deal_ref.1) | copy-start | bytes 1540
  2.9 0.7 %copy-start.1 = (f32[2,1,128]{2,1,0:T(1,128)S(1)}, f32[2,1,128]{2,1,0:T(1,128)}, u32[]{:S(2)}) copy-start(f32[2,1,128]{2,1,0:T(1,128)} %param.10) | copy-start | bytes 3076
  2.9 0.7 %copy-start.2 = (s32[1,128]{1,0:T(1,128)S(1)}, s32[1,128]{1,0:T(1,128)}, u32[]{:S(2)}) copy-start(s32[1,128]{1,0:T(1,128)} %mask_ref.1) | copy-start | bytes 1540
  2.9 4.1 %collective-permute-start.4 = (f32[480,128]{1,0:T(8,128)S(1)}, f32[480,128]{1,0:T(8,128)S(1)}, u32[]{:S(2)}, u32[]{:S(2)}) collective-permute-start(f32[480,128]{1,0:T(8,128)S(1)} %get-tuple-element.28), channel_id=1, source_target_pairs={{0,1},{1,0},{2,3},{3,2},{4,5},{5,4},{6,7},{7,6},{8,9},{9,8},{10,11... | collective-permute-start | bytes 737288 | tf_op jit(solution)/shard_map/ppermute | solution.py:757
  3.6 3.4 %copy-start.4 = (f32[4,12,8,128]{3,2,1,0:T(8,128)S(1)}, f32[4,12,8,128]{3,2,1,0:T(8,128)}, u32[]{:S(2)}) copy-start(f32[4,12,8,128]{3,2,1,0:T(8,128)} %constant.28.clone.angle_ref) | copy-start | bytes 589828
  3.6 3.4 %copy-start.6 = (f32[5,40,128]{2,1,0:T(8,128)S(1)}, f32[5,40,128]{2,1,0:T(8,128)}, u32[]{:S(2)}) copy-start(f32[5,40,128]{2,1,0:T(8,128)} %constant.27.clone.table_ref) | copy-start | bytes 307204
  3.9 3.1 %collective-permute-start = (f32[376,128]{1,0:T(8,128)S(1)}, f32[376,128]{1,0:T(8,128)S(1)}, u32[]{:S(2)}, u32[]{:S(2)}) collective-permute-start(f32[376,128]{1,0:T(8,128)S(1)} %get-tuple-element.22), channel_id=1, source_target_pairs={{0,1},{1,0},{2,3},{3,2},{4,5},{5,4},{6,7},{7,6},{8,9},{9,8},{10,11... | collective-permute-start | bytes 577544 | tf_op jit(solution)/shard_map/ppermute | solution.py:757
  4.4 5.1 %collective-permute-start.1 = (f32[184,128]{1,0:T(8,128)S(1)}, f32[184,128]{1,0:T(8,128)S(1)}, u32[]{:S(2)}, u32[]{:S(2)}) collective-permute-start(f32[184,128]{1,0:T(8,128)S(1)} %get-tuple-element.24), channel_id=1, source_target_pairs={{0,16},{1,2},{2,1},{3,4},{4,3},{5,6},{6,5},{7,8},{8,7},{9,10},{10,... | collective-permute-start | bytes 282632 | tf_op jit(solution)/shard_map/ppermute | solution.py:760
  7.0 2.5 %copy-start.5 = (f32[4,9,8,128]{3,2,1,0:T(8,128)S(1)}, f32[4,9,8,128]{3,2,1,0:T(8,128)}, u32[]{:S(2)}) copy-start(f32[4,9,8,128]{3,2,1,0:T(8,128)} %constant.29.clone.angle_ref) | copy-start | bytes 442372
  7.2 8.0 %collective-permute-start.5 = (f32[40,128]{1,0:T(8,128)S(1)}, f32[40,128]{1,0:T(8,128)S(1)}, u32[]{:S(2)}, u32[]{:S(2)}) collective-permute-start(f32[40,128]{1,0:T(8,128)S(1)} %get-tuple-element.29.refs_3_), channel_id=1, source_target_pairs={{0,1},{1,0},{2,3},{3,2},{4,5},{5,4},{6,7},{7,6},{8,9},{9,8},{10,11... | collective-permute-start | bytes 61448 | tf_op jit(solution)/shard_map/ppermute | solution.py:757
  13.2 4.6 %collective-permute-start.3 = (f32[184,128]{1,0:T(8,128)S(1)}, f32[184,128]{1,0:T(8,128)S(1)}, u32[]{:S(2)}, u32[]{:S(2)}) collective-permute-start(f32[184,128]{1,0:T(8,128)S(1)} %get-tuple-element.26), channel_id=1, source_target_pairs={{0,16},{1,2},{2,1},{3,4},{4,3},{5,6},{6,5},{7,8},{8,7},{9,10},{10,... | collective-permute-start | bytes 282632 | tf_op jit(solution)/shard_map/ppermute | solution.py:760
  15.2 2.6 %collective-permute-start.2 = (f32[184,128]{1,0:T(8,128)S(1)}, f32[184,128]{1,0:T(8,128)S(1)}, u32[]{:S(2)}, u32[]{:S(2)}) collective-permute-start(f32[184,128]{1,0:T(8,128)S(1)} %get-tuple-element.26), channel_id=1, source_target_pairs={{0,1},{1,0},{2,3},{3,2},{4,5},{5,4},{6,7},{7,6},{8,9},{9,8},{10,11... | collective-permute-start | bytes 282632 | tf_op jit(solution)/shard_map/ppermute | solution.py:757
  21.9 8.3 %collective-permute-start.6 = (f32[840,128]{1,0:T(8,128)S(1)}, f32[840,128]{1,0:T(8,128)S(1)}, u32[]{:S(2)}, u32[]{:S(2)}) collective-permute-start(f32[840,128]{1,0:T(8,128)S(1)} %get-tuple-element.34.two_ref), channel_id=1, source_target_pairs={{0,1},{1,0},{2,3},{3,2},{4,5},{5,4},{6,7},{7,6},{8,9},{9,8},{10,11... | collective-permute-start | bytes 1290248 | tf_op jit(solution)/shard_map/ppermute | solution.py:757
  21.9 14.7 %all-to-all-start = ((f32[16,1,128]{2,1,0:T(1,128)}), f32[16,1,128]{2,1,0:T(1,128)S(1)}, u32[]{:S(2)}, u32[]{:S(2)}) async-start(f32[16,1,128]{2,1,0:T(1,128)} %bitcast.5), calls=%async_computation | async-start | bytes 16384 | tf_op jit(solution)/shard_map/all_to_all | solution.py:830
